TPU v7x, 512 devices: a whole 4x8x8 slice. The times are simulated.
512 devices in a mesh: row: 32 (over y, x), col: 16 (over z, core).
Axes of the slice: x: 4, y: 8, z: 8, core: 2. Of those that a mesh axis runs over, the one named last changes fastest.
Arguments:
- source_features: bfloat16 [16, 2048, 256], P('col', 'row'), may hold values from -500 to 500
- target_features: bfloat16 [32768, 256], P(('row', 'col')), may hold values from -6 to 6
- weight: bfloat16 [256, 256], replicated, may hold values from -0.375 to 0.375
- score_source: float32 [4, 64], replicated, may hold values from -0.75 to 0.75
- score_target: float32 [4, 64], replicated, may hold values from -0.75 to 0.75
- out_bias: float32 [256], replicated, may hold values from -3 to 3
- block_list: int32 [32, 16, 48], P('row', 'col'), may hold values from 0 to 127, as said below
- block_count: int32 [32, 16], P('row', 'col'), may hold values from 8 to 48, as said below
- edge_bits: int32 [32, 16, 48, 16, 128], P('row', 'col'), may hold values from 0 to 255, as said below
Outputs:
- updated: bfloat16 [32768, 256], P(('row', 'col'))
Inputs may be any that keep to these rules, and one draw needn't show every extreme that they name: `block_list`: slot s of tile (r, c) names target block p // 16 and source block p % 16 of the tile; the first block_count[r, c] slots of a tile name distinct blocks and later slots are unused. `block_count`: some tile holds 48 blocks. `edge_bits`: bit b of entry [r, c, s, w, i] marks the edge from source 8 w + b to target i of the block in slot s. Some targets have no edge.
All inputs are finite; a program needn't handle non-finite values.
Results may differ from a plain program's by a relative error of at most 0.007.
The roundings to bfloat16 on the way count: a program that leaves them out, or rounds other values in their place, can miss the bound.
Values may be sent and summed in bfloat16 or wider, within the bound.
A program may use at most 64 MiB of HBM per device.

v0:
```python
import jax
import jax.numpy as jnp
from jax import lax
from jax.sharding import PartitionSpec as P

BLK = 128
SB = 16
very_low = -1e30
slope = 0.2


def unpack_all(packed):
    shifts = jnp.arange(8, dtype=jnp.int32)
    spread = jnp.right_shift(packed[:, :, None, :], shifts[None, None, :, None]) & 1
    return spread.reshape(packed.shape[0], packed.shape[1] * 8, packed.shape[2]) > 0


def all_scores(src_pick, dst_pick):
    raw = src_pick[:, :, :, None] + dst_pick[:, :, None, :]
    return jnp.where(raw > 0, raw, slope * raw)


def body(
    source_features,
    target_features,
    weight,
    score_source,
    score_target,
    out_bias,
    block_list,
    block_count,
    edge_bits,
):
    head_count = score_source.shape[0]
    head_size = score_source.shape[1]
    out_width = weight.shape[1]
    own_proj = jnp.dot(source_features[0], weight, preferred_element_type=jnp.float32).astype(
        jnp.bfloat16
    )
    projected = lax.all_gather(own_proj, "row", axis=0, tiled=True)
    src_logits = jnp.einsum(
        "nhk,hk->hn",
        projected.reshape(-1, head_count, head_size).astype(jnp.float32),
        score_source,
        precision=lax.Precision.HIGHEST,
    )
    dst_proj = jnp.dot(target_features, weight, preferred_element_type=jnp.float32)
    dst_local = jnp.einsum(
        "nhk,hk->hn",
        dst_proj.reshape(-1, head_count, head_size),
        score_target,
        precision=lax.Precision.HIGHEST,
    )
    dst_logits = lax.all_gather(dst_local, "col", axis=1, tiled=True)
    dst_rows = dst_logits.shape[1]
    dst_blocks_all = dst_rows // BLK
    src_blocks_all = src_logits.shape[1] // BLK
    slots = block_list[0, 0]
    live = block_count[0, 0]
    packed = edge_bits[0, 0]
    slot_count = slots.shape[0]
    dst_block = slots // SB
    src_block = slots % SB
    in_use = jnp.arange(slot_count, dtype=jnp.int32) < live
    edge_mask = unpack_all(packed) & in_use[:, None, None]
    src_pick = jnp.take(src_logits.reshape(head_count, src_blocks_all, BLK), src_block, axis=1)
    dst_pick = jnp.take(dst_logits.reshape(head_count, dst_blocks_all, BLK), dst_block, axis=1)
    owner = dst_block[:, None] == jnp.arange(dst_blocks_all, dtype=jnp.int32)[None, :]
    owner_float = owner.astype(jnp.float32)
    scores = all_scores(src_pick, dst_pick)
    block_max = jnp.max(jnp.where(edge_mask[None], scores, very_low), axis=2)
    spread_max = jnp.where(owner[None, :, :, None], block_max[:, :, None, :], very_low)
    row_max = jnp.max(spread_max, axis=1).reshape(head_count, dst_rows)
    row_max = lax.pmax(row_max, "col")
    prior_max = jnp.take(row_max.reshape(head_count, dst_blocks_all, BLK), dst_block, axis=1)
    scores = all_scores(src_pick, dst_pick)
    numer = jnp.exp(jnp.where(edge_mask[None], scores - prior_max[:, :, None, :], very_low))
    slot_denoms = jnp.sum(numer, axis=2)
    denoms = jnp.einsum(
        "sd,hsi->dih", owner_float, slot_denoms, precision=lax.Precision.HIGHEST
    ).reshape(dst_rows, head_count)
    weights = numer.astype(jnp.bfloat16)
    src_feats = jnp.take(
        projected.reshape(src_blocks_all, BLK, head_count, head_size), src_block, axis=0
    )
    product = jnp.einsum("hsji,sjhk->sihk", weights, src_feats, preferred_element_type=jnp.float32)
    accum = jnp.einsum(
        "sd,sihk->dihk", owner_float, product, precision=lax.Precision.HIGHEST
    ).reshape(dst_rows, out_width)
    accum, denoms = (
        lax.psum(accum.astype(jnp.bfloat16), "col").astype(jnp.float32),
        lax.psum(denoms.astype(jnp.bfloat16), "col").astype(jnp.float32),
    )
    own_count = dst_rows // lax.axis_size("col")
    first_row = lax.axis_index("col") * own_count
    accum = lax.dynamic_slice_in_dim(accum, first_row, own_count, 0)
    denoms = lax.dynamic_slice_in_dim(denoms, first_row, own_count, 0)
    own_count = accum.shape[0]
    blended = accum.reshape(own_count, head_count, head_size) / jnp.maximum(denoms, 1.0)[:, :, None]
    return jax.nn.elu(blended.reshape(own_count, out_width) + out_bias).astype(jnp.bfloat16)


def solution(mesh):
    placed = (
        P("col", "row", None),
        P(("row", "col"), None),
        P(),
        P(),
        P(),
        P(),
        P("row", "col", None),
        P("row", "col"),
        P("row", "col", None, None, None),
    )
    return jax.shard_map(
        body, mesh=mesh, in_specs=placed, out_specs=P(("row", "col"), None), check_vma=False
    )
```

profile of v0, /device:TPU:1, one launch (start us, length us, event | category | flops | bytes accessed | tf_op | source)
XLA Modules:
  0.0 296.6 jit_solution(9279656370350139183)
XLA Ops:
  6.5 0.0 copy-start
  6.5 0.0 all-gather.3.cloned.1.call-start
  6.5 0.9 copy-done
  7.4 1.5 convolution_convert_fusion
  9.0 0.0 all-gather.3.cloned.1.call-update
  9.0 0.0 all-reduce.2.cloned.1.call-start
  9.0 0.9 fusion.45
  9.9 0.1 reshape.177
  10.1 1.0 fusion.28
  11.1 24.6 %all-gather = f32[16,64,4]{1,2,0:T(4,128)S(1)} all-gather(f32[1,64,4]{1,2,0:T(4,128)S(1)} %bitcast.101), channel_id=1, replica_groups=mesh['row'=32,'col'=16] {'col'}, dimensions={0}, use_global_device_ids=true | all-gather | bytes 17408 | tf_op jit(solution)/shard_map/all_gather | solution.py:54
  35.6 0.1 reshape.217
  35.7 0.1 shift_right_arithmetic.30
  36.5 0.7 compare_and_fusion
  37.2 0.1 copy.42
  37.3 0.6 gather_fusion.2
  37.9 0.7 fusion.39
  38.6 1.9 fusion.17
  40.6 0.0 copy-start.2
  40.6 52.5 %all-gather.3.cloned.1.call-done = bf16[2048,256]{1,0:T(8,128)(2,1)} async-done(((bf16[64,256]{1,0:T(8,128)(2,1)}), bf16[2048,256]{1,0:T(8,128)(2,1)}) %all-gather.3.cloned.1.call-update) | async-done | bytes 1048592 | tf_op jit(solution)/shard_map/all_gather | solution.py:40
  93.1 1.6 copy.40
  94.7 1.2 fusion.44
  95.9 0.6 gather_fusion.1
  96.5 0.2 select_bitcast_fusion.1
  96.7 4.4 %select_reduce_fusion = f32[4,48,128]{2,0,1:T(4,128)S(1)} fusion(f32[4,48,128]{2,0,1:T(4,128)S(1)} %get-tuple-element.9, f32[4,48,128]{2,0,1:T(4,128)S(1)} %get-tuple-element.10, pred[48,128,128]{2,1,0:T(8,128)(4,1)S(1)} %fusion.17), kind=kLoop, calls=%fused_computation.6 | loop fusion | flops 18849792 | bytes 1081344 | tf_op jit(solution)/shard_map/reduce_max | solution.py:71
  101.1 0.1 select_reduce_fusion.1
  101.2 48.2 %pmax.7 = f32[4,8,128]{2,0,1:T(4,128)S(1)} all-reduce(f32[4,8,128]{2,0,1:T(4,128)S(1)} %copy.44), channel_id=1, replica_groups=mesh['row'=32,'col'=16] {'col'}, use_global_device_ids=true, to_apply=%region_2.4 | all-reduce | flops 4096 | bytes 32768 | tf_op jit(solution)/shard_map/pmax | solution.py:74
  149.4 0.6 gather_fusion.3
  150.1 0.0 copy-done.2
  150.1 0.8 select_bitcast_fusion
  150.8 0.0 copy-done.1
  150.8 0.8 reshape.228
  151.7 1.1 copy.39
  152.8 2.7 gather_fusion
  155.5 9.9 %fusion.18 = f32[48,128,4,64]{1,3,2,0:T(8,128)S(1)} fusion(f32[4,48,128]{2,0,1:T(4,128)S(1)} %copy-done.4, f32[4,48,128]{2,0,1:T(4,128)S(1)} %get-tuple-element.9, f32[4,48,128]{2,0,1:T(4,128)S(1)} %get-tuple-element.10, pred[48,128,128]{2,1,0:T(8,128)(4,1)S(1)} %copy-done.3, bf16[48,128,4,64]{1,3,2,0:T(8,128)(2,1)} %gather_fusion, ...), kind=kOutput, calls=%fused_computation.25 | convolution fusion | flops 426246144 | bytes 10518576 | tf_op jit(solution)/shard_map/hsji,sjhk->sihk/dot_general | solution.py:86
  165.4 0.0 copy-start.5
  165.4 5.7 %fusion.24 = bf16[8,128,4,64]{1,0,3,2:T(8,128)(2,1)S(1)} fusion(f32[48,128,4,64]{1,3,2,0:T(8,128)S(1)} %fusion.18, s32[48]{0:T(128)S(1)} %get-tuple-element.7), kind=kOutput, calls=%fused_computation.27 | convolution fusion | flops 151257472 | bytes 6815936 | tf_op jit(solution)/shard_map/sd,sihk->dihk/dot_general | solution.py:87
  171.1 0.1 copy.70
  171.2 1.0 copy.46
  172.2 0.0 all-reduce.2.cloned.1.call-update
  172.2 5.5 %fusion = f32[4,48,128]{2,0,1:T(4,128)S(1)} fusion(f32[4,48,128]{2,0,1:T(4,128)S(1)} %copy-done.4, f32[4,48,128]{2,0,1:T(4,128)S(1)} %get-tuple-element.9, f32[4,48,128]{2,0,1:T(4,128)S(1)} %get-tuple-element.10, pred[48,128,128]{2,1,0:T(8,128)(4,1)S(1)} %copy-done.3), kind=kLoop, calls=%fused_computation.7 | loop fusion | flops 21995520 | bytes 1179648 | tf_op jit(solution)/shard_map/reduce_sum | solution.py:78
  177.7 0.2 fusion.27
  177.9 27.0 %psum.15 = bf16[1024,4]{0,1:T(4,128)(2,1)S(1)} all-reduce(bf16[1024,4]{0,1:T(4,128)(2,1)S(1)} %bitcast.100), channel_id=1, replica_groups=mesh['row'=32,'col'=16] {'col'}, use_global_device_ids=true, to_apply=%region_5.7 | all-reduce | flops 4096 | bytes 16384 | tf_op jit(solution)/shard_map/psum | solution.py:92
  204.9 0.1 convert_maximum_fusion
  205.0 0.1 copy.48
  205.1 0.1 div.27
  205.2 0.1 div.28
  205.4 83.0 %all-reduce.2.cloned.1.call-done = bf16[1024,256]{1,0:T(8,128)(2,1)} async-done(((bf16[1024,256]{1,0:T(8,128)(2,1)}), bf16[1024,256]{1,0:T(8,128)(2,1)}) %all-reduce.2.cloned.1.call-update) | async-done | bytes 524304 | tf_op jit(solution)/shard_map/psum | solution.py:91
  288.3 1.4 fusion.32
  (17 shorter events, 0.1 us)
Async XLA Ops:
  6.5 0.9 copy-start
  6.5 86.5 %all-gather.3.cloned.1.call-start = ((), (), s32[]{:S(2)}) async-start(), calls=%async_computation | async-start | bytes 1081344 | tf_op jit(solution)/shard_map/all_gather | solution.py:40
  9.0 279.3 %all-reduce.2.cloned.1.call-start = ((), (), s32[]{:S(2)}) async-start(), calls=%async_computation.1 | async-start | bytes 1048576 | tf_op jit(solution)/shard_map/psum | solution.py:91
  40.6 109.5 %copy-start.2 = (pred[48,128,128]{2,1,0:T(8,128)(4,1)}, pred[48,128,128]{2,1,0:T(8,128)(4,1)S(1)}, u32[]{:S(2)}) copy-start(pred[48,128,128]{2,1,0:T(8,128)(4,1)S(1)} %fusion.17) | copy-start | bytes 2359300
  93.1 57.7 %copy-start.1 = (bf16[2048,256]{1,0:T(8,128)(2,1)S(1)}, bf16[2048,256]{1,0:T(8,128)(2,1)}, u32[]{:S(2)}) copy-start(bf16[2048,256]{1,0:T(8,128)(2,1)} %all-gather.3.cloned.1.call-done) | copy-start | bytes 3145732
  152.8 2.7 copy-start.3
  152.8 2.7 copy-start.4
  165.4 122.9 %copy-start.5 = (f32[256]{0:T(256)S(1)}, f32[256]{0:T(256)}, u32[]{:S(2)}) copy-start(f32[256]{0:T(256)} %param.16) | copy-start | bytes 3076
Sparse Core Ops, SparseCore 0:
  10.5 82.5 all-gather.2
  172.3 115.9 all-reduce.1
where the time goes:
time: 297 us
  waiting for transfers between devices  136 us (46%)
  blocking collectives  99.8 us (34%)
  matrix products  20.3 us (7%)
  other arithmetic  15.7 us (5%)
  between operations  14.3 us (5%)
  local copies, waits for them, and re-layouts  10.9 us (4%)
    psum x1, waiting for transfers between devices, body(): lax.psum(accum.astype(jnp.bfloat16), 'col').astype(jnp.float32)  83 us
    all_gather x1, waiting for transfers between devices, body(): projected = lax.all_gather(own_proj, 'row', axis=0, tiled=True)  52.5 us
    pmax x1, blocking collectives, body(): row_max = lax.pmax(row_max, 'col')  48.2 us
    psum x1, blocking collectives, body(): lax.psum(denoms.astype(jnp.bfloat16), 'col').astype(jnp.float32)  27 us
    all_gather x1, blocking collectives, body(): dst_logits = lax.all_gather(dst_local, 'col', axis=1, tiled=True)  24.6 us
    dot_general x1, matrix products, body(): jnp.einsum('hsji,sjhk->sihk', weights, src_feats, preferred_element_type=...  9.89 us
  transfers between devices with their start and end apart: 2, of which 2 were waited for; matrix products, arithmetic and copies ran while one was open for 4% of the time, Pallas kernels for 0%

commit v1 on v0

--- a/solution.py
+++ b/solution.py
@@ -37,7 +37,11 @@
     own_proj = jnp.dot(source_features[0], weight, preferred_element_type=jnp.float32).astype(
         jnp.bfloat16
     )
-    projected = lax.all_gather(own_proj, "row", axis=0, tiled=True)
+    size = lax.axis_size("row")
+    repeats = [size if d == 0 else 1 for d in range(own_proj.ndim)]
+    projected = lax.all_to_all(
+        jnp.tile(own_proj, repeats), "row", split_axis=0, concat_axis=0, tiled=True
+    )
     src_logits = jnp.einsum(
         "nhk,hk->hn",
         projected.reshape(-1, head_count, head_size).astype(jnp.float32),

time: 297 us -> 253 us (0.85)
  waiting for transfers between devices: 136 us -> 80.1 us
  starting transfers between devices: 0.04 us -> 10.5 us
    all_gather x1 -> x0, waiting for transfers between devices: 52.5 us -> none  [body(): projected = lax.all_gather(own_proj, 'row', axis=0, tiled=True)]
    all_to_all x0 -> x1, starting transfers between devices: none -> 10.5 us  [body(): lax.all_to_all(jnp.tile(own_proj, repeats), 'row', split_axis=0, concat_a...]
  transfers between devices with their start and end apart: 2 -> 2, of which waited for: 2 -> 1; matrix products, arithmetic and copies ran while one was open for 4% -> 5% of each run, Pallas kernels for 0% -> 0%
where the time goes in v1:
time: 253 us; the launch traced here: 252 us
  blocking collectives  97.3 us (38%)
  waiting for transfers between devices  80.1 us (32%)
  matrix products  21.8 us (9%)
  other arithmetic  15.7 us (6%)
  between operations  14.3 us (6%)
  local copies, waits for them, and re-layouts  12.4 us (5%)
  starting transfers between devices  10.5 us (4%)
    psum x1, waiting for transfers between devices, body(): lax.psum(accum.astype(jnp.bfloat16), 'col').astype(jnp.float32)  80 us
    pmax x1, blocking collectives, body(): row_max = lax.pmax(row_max, 'col')  46.3 us
    psum x1, blocking collectives, body(): lax.psum(denoms.astype(jnp.bfloat16), 'col').astype(jnp.float32)  26.9 us
    all_gather x1, blocking collectives, body(): dst_logits = lax.all_gather(dst_local, 'col', axis=1, tiled=True)  24 us
    all_to_all x1, starting transfers between devices, body(): lax.all_to_all(jnp.tile(own_proj, repeats), 'row', split_axis=0, concat_a...  10.5 us
    dot_general x1, matrix products, body(): jnp.einsum('hsji,sjhk->sihk', weights, src_feats, preferred_element_type=...  9.89 us
    dot_general x1, matrix products, body(): jnp.einsum('sd,sihk->dihk', owner_float, product, precision=lax.Precision...  5.67 us
    reduce_sum x1, other arithmetic, body(): slot_denoms = jnp.sum(numer, axis=2)  5.5 us
  transfers between devices with their start and end apart: 2, of which 1 were waited for; matrix products, arithmetic and copies ran while one was open for 5% of the time, Pallas kernels for 0%

profile of v1, /device:TPU:1, one launch (start us, length us, event | category | flops | bytes accessed | tf_op | source)
XLA Modules:
  0.0 252.1 jit_solution(1095672618639681363)
XLA Ops:
  6.5 0.0 copy-start
  6.5 0.9 copy-done
  7.4 0.9 convolution_convert_fusion
  8.3 1.1 tile.2
  9.5 10.5 %all-to-all-start = ((bf16[32,64,256]{2,1,0:T(8,128)(2,1)}), bf16[32,64,256]{2,1,0:T(8,128)(2,1)S(1)}, u32[]{:S(2)}, u32[]{:S(2)}) async-start(bf16[32,64,256]{2,1,0:T(8,128)(2,1)} %tile.2), calls=%async_computation | async-start | bytes 2097152 | tf_op jit(solution)/shard_map/all_to_all | solution.py:42
  20.0 0.0 all-reduce.2.cloned.1.call-start
  20.0 0.9 fusion.46
  20.9 0.1 reshape.186
  21.1 1.0 fusion.30
  22.0 24.0 %all-gather = f32[16,64,4]{1,2,0:T(4,128)S(1)} all-gather(f32[1,64,4]{1,2,0:T(4,128)S(1)} %bitcast.98), channel_id=1, replica_groups=mesh['row'=32,'col'=16] {'col'}, dimensions={0}, use_global_device_ids=true | all-gather | bytes 17408 | tf_op jit(solution)/shard_map/all_gather | solution.py:58
  46.1 0.1 reshape.226
  46.2 0.1 shift_right_arithmetic.30
  46.9 0.7 compare_and_fusion
  47.6 0.1 copy.40
  47.7 0.6 gather_fusion.2
  48.4 0.7 fusion.41
  49.0 1.9 fusion.17
  51.0 0.0 copy-start.1
  51.0 0.0 all-to-all-done
  51.0 1.9 reshape.238
  52.9 0.0 copy-done.5
  52.9 3.3 %fusion.23 = f32[4,1,2048]{2,1,0:T(1,128)S(1)} fusion(f32[4,64,1]{1,2,0:T(1,128)S(1)} %bitcast.100, bf16[2048,4,64]{2,1,0:T(4,128)(2,1)} %reshape.238), kind=kOutput, calls=%fused_computation.26 | convolution fusion | flops 6291456 | bytes 1082368 | tf_op jit(solution)/shard_map/nhk,hk->hn/dot_general | solution.py:45
  56.2 0.6 gather_fusion.1
  56.8 0.2 select_bitcast_fusion.1
  57.0 4.4 %select_reduce_fusion = f32[4,48,128]{2,0,1:T(4,128)S(1)} fusion(f32[4,48,128]{2,0,1:T(4,128)S(1)} %get-tuple-element.9, f32[4,48,128]{2,0,1:T(4,128)S(1)} %get-tuple-element.10, pred[48,128,128]{2,1,0:T(8,128)(4,1)S(1)} %fusion.17), kind=kLoop, calls=%fused_computation.6 | loop fusion | flops 18849792 | bytes 1081344 | tf_op jit(solution)/shard_map/reduce_max | solution.py:75
  61.4 0.1 select_reduce_fusion.1
  61.6 46.3 %pmax.7 = f32[4,8,128]{2,0,1:T(4,128)S(1)} all-reduce(f32[4,8,128]{2,0,1:T(4,128)S(1)} %copy.42), channel_id=1, replica_groups=mesh['row'=32,'col'=16] {'col'}, use_global_device_ids=true, to_apply=%region_2.4 | all-reduce | flops 4096 | bytes 32768 | tf_op jit(solution)/shard_map/pmax | solution.py:78
  107.9 0.6 gather_fusion.3
  108.6 0.8 select_bitcast_fusion
  109.3 0.8 reshape.237
  110.1 1.1 copy.37
  111.3 2.7 %gather_fusion = bf16[48,128,4,64]{1,3,2,0:T(8,128)(2,1)} fusion(bf16[16,128,4,64]{1,3,2,0:T(8,128)(2,1)S(1)} %copy.37, s32[1024]{0:T(1024)S(1)} %pad_clamp_fusion.1), kind=kCustom, calls=%fused_computation.2 | custom fusion | bytes 6291648 | tf_op jit(solution)/shard_map/jit(_take)/gather | solution.py:87
  114.0 0.0 copy-done.2
  114.0 9.9 %fusion.18 = f32[48,128,4,64]{1,3,2,0:T(8,128)S(1)} fusion(f32[4,48,128]{2,0,1:T(4,128)S(1)} %copy-done.3, f32[4,48,128]{2,0,1:T(4,128)S(1)} %get-tuple-element.9, f32[4,48,128]{2,0,1:T(4,128)S(1)} %get-tuple-element.10, pred[48,128,128]{2,1,0:T(8,128)(4,1)S(1)} %copy-done.2, bf16[48,128,4,64]{1,3,2,0:T(8,128)(2,1)} %gather_fusion, ...), kind=kOutput, calls=%fused_computation.25 | convolution fusion | flops 426246144 | bytes 10518576 | tf_op jit(solution)/shard_map/hsji,sjhk->sihk/dot_general | solution.py:90
  123.9 0.0 copy-start.4
  123.9 5.7 %fusion.26 = bf16[8,128,4,64]{1,0,3,2:T(8,128)(2,1)S(1)} fusion(f32[48,128,4,64]{1,3,2,0:T(8,128)S(1)} %fusion.18, s32[48]{0:T(128)S(1)} %get-tuple-element.7), kind=kOutput, calls=%fused_computation.29 | convolution fusion | flops 151257472 | bytes 6815936 | tf_op jit(solution)/shard_map/sd,sihk->dihk/dot_general | solution.py:91
  129.6 0.1 copy.71
  129.7 1.0 copy.44
  130.7 0.0 all-reduce.2.cloned.1.call-update
  130.7 5.5 %fusion = f32[4,48,128]{2,0,1:T(4,128)S(1)} fusion(f32[4,48,128]{2,0,1:T(4,128)S(1)} %copy-done.3, f32[4,48,128]{2,0,1:T(4,128)S(1)} %get-tuple-element.9, f32[4,48,128]{2,0,1:T(4,128)S(1)} %get-tuple-element.10, pred[48,128,128]{2,1,0:T(8,128)(4,1)S(1)} %copy-done.2), kind=kLoop, calls=%fused_computation.7 | loop fusion | flops 21995520 | bytes 1179648 | tf_op jit(solution)/shard_map/reduce_sum | solution.py:82
  136.2 0.2 fusion.29
  136.4 26.9 %psum.15 = bf16[1024,4]{0,1:T(4,128)(2,1)S(1)} all-reduce(bf16[1024,4]{0,1:T(4,128)(2,1)S(1)} %bitcast.97), channel_id=1, replica_groups=mesh['row'=32,'col'=16] {'col'}, use_global_device_ids=true, to_apply=%region_5.7 | all-reduce | flops 4096 | bytes 16384 | tf_op jit(solution)/shard_map/psum | solution.py:96
  163.3 0.1 convert_maximum_fusion
  163.4 0.1 copy.46
  163.5 0.1 div.27
  163.6 0.1 div.28
  163.8 80.0 %all-reduce.2.cloned.1.call-done = bf16[1024,256]{1,0:T(8,128)(2,1)} async-done(((bf16[1024,256]{1,0:T(8,128)(2,1)}), bf16[1024,256]{1,0:T(8,128)(2,1)}) %all-reduce.2.cloned.1.call-update) | async-done | bytes 524304 | tf_op jit(solution)/shard_map/psum | solution.py:95
  243.8 1.4 fusion.34
  (17 shorter events, 0.1 us)
Async XLA Ops:
  6.5 0.9 copy-start
  6.5 46.3 %copy-start.5 = (f32[4,64]{1,0:T(4,128)S(1)}, f32[4,64]{1,0:T(4,128)}, u32[]{:S(2)}) copy-start(f32[4,64]{1,0:T(4,128)} %param.14) | copy-start | bytes 3076
  9.5 41.5 %all-to-all-start = ((bf16[32,64,256]{2,1,0:T(8,128)(2,1)}), bf16[32,64,256]{2,1,0:T(8,128)(2,1)S(1)}, u32[]{:S(2)}, u32[]{:S(2)}) async-start(bf16[32,64,256]{2,1,0:T(8,128)(2,1)} %tile.2), calls=%async_computation | async-start | bytes 2097152 | tf_op jit(solution)/shard_map/all_to_all | solution.py:42
  20.0 223.8 %all-reduce.2.cloned.1.call-start = ((), (), s32[]{:S(2)}) async-start(), calls=%async_computation.1 | async-start | bytes 1048576 | tf_op jit(solution)/shard_map/psum | solution.py:95
  51.0 57.6 %copy-start.1 = (pred[48,128,128]{2,1,0:T(8,128)(4,1)}, pred[48,128,128]{2,1,0:T(8,128)(4,1)S(1)}, u32[]{:S(2)}) copy-start(pred[48,128,128]{2,1,0:T(8,128)(4,1)S(1)} %fusion.17) | copy-start | bytes 2359300
  111.2 2.7 %copy-start.2 = (pred[48,128,128]{2,1,0:T(8,128)(4,1)S(1)}, pred[48,128,128]{2,1,0:T(8,128)(4,1)}, u32[]{:S(2)}) copy-start(pred[48,128,128]{2,1,0:T(8,128)(4,1)} %copy-done.1) | copy-start | bytes 2359300
  111.2 2.7 %copy-start.3 = (f32[4,48,128]{2,0,1:T(4,128)S(1)}, f32[4,48,128]{2,0,1:T(4,128)}, u32[]{:S(2)}) copy-start(f32[4,48,128]{2,0,1:T(4,128)} %select_bitcast_fusion) | copy-start | bytes 294916
  123.9 119.9 %copy-start.4 = (f32[256]{0:T(256)S(1)}, f32[256]{0:T(256)}, u32[]{:S(2)}) copy-start(f32[256]{0:T(256)} %param.16) | copy-start | bytes 3076
Sparse Core Ops, SparseCore 0:
  130.8 112.9 all-reduce.1
